TPU v7x, 32 devices: a whole 2x2x4 slice. The times are simulated.
32 devices in a mesh: cuts: 2 (over y), leg: 8 (over z, x), sub: 2 (over core).
Axes of the slice: x: 2, y: 2, z: 4, core: 2. Of those that a mesh axis runs over, the one named last changes fastest.
Arguments:
- stem_tensor: bfloat16 [2, 32768, 512], P(None, ('cuts', 'leg', 'sub')), parts along dimension 1, may hold values from -6 to 6
- branches: bfloat16 [3, 2, 2, 512, 512], P(None, None, None, 'leg', 'sub'), may hold values from -0.1875 to 0.1875
- contraction_order: int32 [3], replicated, may hold values from 0 to 2, each once
- cut_values: int32 [6], P('cuts'), parts along dimension 0, may hold values from 0 to 1
Outputs:
- contracted: bfloat16 [2, 32768, 512], P(None, ('cuts', 'leg', 'sub')), parts along dimension 1
There are 2 independent parts, one for each index of `cuts`. A program takes and returns all parts, laid end to end along the dimension named above; an argument that names none is the same for every part. Nothing has to cross between parts.
Inputs may be any that keep to these rules, and one draw needn't show every extreme that they name: `contraction_order`: a permutation of 0 to 2.
All inputs are finite; a program needn't handle non-finite values.
Results may differ from a plain program's by a relative error of at most 0.0058.
Values may be sent and summed in bfloat16 or wider, within the bound.
A program may use at most 64 MiB of HBM per device.

v0:
```python
import jax
import jax.numpy as jnp
from jax import lax
from jax.sharding import PartitionSpec as P

STEPS = 3


def permute_legs(flat, high_bits, low_size, rotation):
    lead = flat.shape[:-1]
    lead_count = len(lead)
    split = flat.reshape(lead + (2,) * high_bits + (low_size,))
    axes = list(range(lead_count))
    for dest_pos in range(high_bits):
        dest_bit = high_bits - 1 - dest_pos
        source_bit = (dest_bit + rotation) % high_bits
        axes.append(lead_count + high_bits - 1 - source_bit)
    axes.append(lead_count + high_bits)
    return jnp.transpose(split, axes).reshape(flat.shape)


def complex_matrix(complex_block):
    real_part = complex_block[0]
    imag_part = complex_block[1]
    upper = jnp.concatenate([real_part, imag_part], 1)
    lower = jnp.concatenate([-imag_part, real_part], 1)
    return jnp.concatenate([upper, lower], 0)


def fold_rows(stem_rows, shard_piece):
    operand = jnp.concatenate([stem_rows[0], stem_rows[1]], 1)
    return jnp.dot(operand, complex_matrix(shard_piece), preferred_element_type=jnp.float32)


def shards(stem_tensor, branches, contraction_order, cut_values):
    row_count = stem_tensor.shape[1]
    col_count = stem_tensor.shape[2]
    low_size = col_count // 4
    high_bits = (row_count * col_count // low_size).bit_length() - 1
    leg_count = lax.axis_size("leg")
    core_count = lax.axis_size("sub")
    dev_count = leg_count * core_count
    current = stem_tensor
    for section_index in range(STEPS):
        flattened = current.reshape(2, row_count * col_count)
        permuted = permute_legs(flattened, high_bits, low_size, 2 * section_index + 3)
        blocks = permuted.reshape(2, dev_count, row_count // dev_count, col_count)
        arrived = lax.all_to_all(blocks, ("leg", "sub"), split_axis=1, concat_axis=1, tiled=True)
        regrouped = arrived.reshape(2, row_count, col_count)
        chosen = branches[contraction_order[section_index], cut_values[section_index]]
        branch_part = lax.all_gather(chosen, "sub", axis=2, tiled=True)
        new_width = branch_part.shape[2]
        product = fold_rows(regrouped, lax.all_gather(branch_part, "leg", axis=1, tiled=True))
        current = jnp.stack([product[:, :new_width], product[:, new_width:]]).astype(jnp.bfloat16)
    return current


def solution(mesh):
    placed = (
        P(None, ("cuts", "leg", "sub"), None),
        P(None, None, None, "leg", "sub"),
        P(),
        P("cuts"),
    )
    return jax.shard_map(
        shards,
        mesh=mesh,
        in_specs=placed,
        out_specs=P(None, ("cuts", "leg", "sub"), None),
        check_vma=False,
    )
```

profile of v0, /device:TPU:0, one launch (start us, length us, event | category | flops | bytes accessed | tf_op | source)
XLA Modules:
  0.0 273.1 jit_solution(909891927304989765)
XLA Ops:
  6.5 4.0 %reshape_reshape.14 = bf16[2,2,2,2,2,2,2,2,2,2,2,2,2,128]{13,12,11,10,9,8,7,6,5,4,3,2,1,0:T(2,128)(2,1)} reshape(bf16[2,1024,512]{2,1,0:T(8,128)(2,1)} %param.4) | data formatting | bytes 4194304 | tf_op jit(solution)/shard_map/reshape;reshape | solution.py:12
  10.5 3.9 %copy.19 = bf16[2,2,2,2,2,2,2,2,2,2,2,2,2,128]{13,9,8,7,6,5,4,3,2,1,12,11,10,0:T(2,128)(2,1)S(1)} copy(bf16[2,2,2,2,2,2,2,2,2,2,2,2,2,128]{13,12,11,10,9,8,7,6,5,4,3,2,1,0:T(2,128)(2,1)} %reshape_reshape.14) | data formatting | bytes 4194304 | tf_op jit(solution)/shard_map/reshape;reshape | solution.py:12
  14.4 2.2 reshape_reshape.15
  16.6 3.2 %copy.11 = bf16[2,16,64,512]{3,2,0,1:T(8,128)(2,1)} copy(bf16[2,16,64,512]{3,2,1,0:T(8,128)(2,1)} %reshape_reshape.15) | data formatting | bytes 4194304 | tf_op jit(solution)/shard_map/reshape;reshape | solution.py:47
  19.8 7.5 %all-to-all-start = ((bf16[2,16,64,512]{3,2,0,1:T(8,128)(2,1)}), bf16[2,16,64,512]{3,2,0,1:T(8,128)(2,1)S(1)}, u32[]{:S(2)}, u32[]{:S(2)}) async-start(bf16[2,16,64,512]{3,2,0,1:T(8,128)(2,1)} %copy.11), calls=%async_computation | async-start | bytes 4194304 | tf_op jit(solution)/shard_map/all_to_all | solution.py:48
  40.4 2.1 all-gather
  42.5 51.1 %all-gather.10.cloned.1.call-done = bf16[1,1,2,512,512]{4,3,2,1,0:T(8,128)(2,1)} async-done(((bf16[1,1,2,64,512]{4,3,2,1,0:T(8,128)(2,1)}), bf16[1,1,2,512,512]{4,3,2,1,0:T(8,128)(2,1)}) %all-gather.10.cloned.1.call-update) | async-done | bytes 1048592 | tf_op jit(solution)/shard_map/all_gather | solution.py:53
  94.7 2.1 slice_bitcast_fusion.6
  97.8 2.3 fusion.43
  103.3 3.0 %maximum_bitcast_fusion = bf16[2,2,2,2,2,2,2,2,2,2,2,2,2,128]{13,12,11,10,9,8,7,6,5,4,3,2,1,0:T(2,128)(2,1)S(1)} fusion(bf16[1,2,2,2,2,2,2,2,2,2,2,2,2,128]{13,7,6,5,4,3,2,1,12,11,10,9,8,0:T(2,128)(2,1)S(1)} %copy.13, bf16[1,2,2,2,2,2,2,2,2,2,2,2,2,128]{13,7,6,5,4,3,2,1,12,11,10,9,8,0:T(2,128)(2,1)S(1)} %copy.12), kind=kLoop, calls=%fused_computation.11 | loop fusion | flops 1048576 | bytes 4194304 | tf_op jit(solution)/shard_map/transpose | solution.py:19
  106.3 2.2 reshape_reshape.16
  108.5 3.2 %copy.14 = bf16[2,16,64,512]{3,2,0,1:T(8,128)(2,1)} copy(bf16[2,16,64,512]{3,2,1,0:T(8,128)(2,1)} %reshape_reshape.16) | data formatting | bytes 4194304 | tf_op jit(solution)/shard_map/reshape;reshape | solution.py:47
  111.7 3.7 %all-to-all-start.1 = ((bf16[2,16,64,512]{3,2,0,1:T(8,128)(2,1)}), bf16[2,16,64,512]{3,2,0,1:T(8,128)(2,1)S(1)}, u32[]{:S(2)}, u32[]{:S(2)}) async-start(bf16[2,16,64,512]{3,2,0,1:T(8,128)(2,1)} %copy.14), calls=%async_computation.1 | async-start | bytes 4194304 | tf_op jit(solution)/shard_map/all_to_all | solution.py:48
  115.4 2.2 all-gather.2
  117.7 58.4 %all-gather.12.cloned.1.call-done = bf16[1,1,2,512,512]{4,3,2,1,0:T(8,128)(2,1)} async-done(((bf16[1,1,2,64,512]{4,3,2,1,0:T(8,128)(2,1)}), bf16[1,1,2,512,512]{4,3,2,1,0:T(8,128)(2,1)}) %all-gather.12.cloned.1.call-update) | async-done | bytes 1048592 | tf_op jit(solution)/shard_map/all_gather | solution.py:53
  177.1 2.1 slice_bitcast_fusion.4
  180.2 2.3 fusion.38
  185.5 3.0 %maximum_bitcast_fusion.1 = bf16[2,2,2,2,2,2,2,2,2,2,2,2,2,128]{13,12,11,10,9,8,7,6,5,4,3,2,1,0:T(2,128)(2,1)S(1)} fusion(bf16[1,2,2,2,2,2,2,2,2,2,2,2,2,128]{13,5,4,3,2,1,12,11,10,9,8,7,6,0:T(2,128)(2,1)S(1)} %copy.16, bf16[1,2,2,2,2,2,2,2,2,2,2,2,2,128]{13,5,4,3,2,1,12,11,10,9,8,7,6,0:T(2,128)(2,1)S(1)} %copy.15), kind=kLoop, calls=%fused_computation.23 | loop fusion | flops 1048576 | bytes 4194304 | tf_op jit(solution)/shard_map/transpose | solution.py:19
  188.4 2.2 reshape_reshape.17
  190.7 3.2 %copy.17 = bf16[2,16,64,512]{3,2,0,1:T(8,128)(2,1)} copy(bf16[2,16,64,512]{3,2,1,0:T(8,128)(2,1)} %reshape_reshape.17) | data formatting | bytes 4194304 | tf_op jit(solution)/shard_map/reshape;reshape | solution.py:47
  193.8 3.9 %all-to-all-start.2 = ((bf16[2,16,64,512]{3,2,0,1:T(8,128)(2,1)}), bf16[2,16,64,512]{3,2,0,1:T(8,128)(2,1)S(1)}, u32[]{:S(2)}, u32[]{:S(2)}) async-start(bf16[2,16,64,512]{3,2,0,1:T(8,128)(2,1)} %copy.17), calls=%async_computation.2 | async-start | bytes 4194304 | tf_op jit(solution)/shard_map/all_to_all | solution.py:48
  197.8 2.1 all-gather.4
  199.9 58.5 %all-gather.14.cloned.1.call-done = bf16[1,1,2,512,512]{4,3,2,1,0:T(8,128)(2,1)} async-done(((bf16[1,1,2,64,512]{4,3,2,1,0:T(8,128)(2,1)}), bf16[1,1,2,512,512]{4,3,2,1,0:T(8,128)(2,1)}) %all-gather.14.cloned.1.call-update) | async-done | bytes 1048592 | tf_op jit(solution)/shard_map/all_gather | solution.py:53
  262.5 2.3 fusion.33
  (43 shorter events, 17.6 us)
Async XLA Ops:
  19.8 7.6 %copy-start.4 = (s32[3]{0:T(128)S(1)}, s32[3]{0:T(128)}, u32[]{:S(2)}) copy-start(s32[3]{0:T(128)} %param.6) | copy-start | bytes 40
  19.8 10.6 %copy-start.5 = (s32[3]{0:T(128)S(1)}, s32[3]{0:T(128)}, u32[]{:S(2)}) copy-start(s32[3]{0:T(128)} %param.7) | copy-start | bytes 40
  19.8 20.6 %copy-start.3 = (bf16[3,2,2,64,256]{4,3,2,1,0:T(8,128)(2,1)S(1)}, bf16[3,2,2,64,256]{4,3,2,1,0:T(8,128)(2,1)}, u32[]{:S(2)}) copy-start(bf16[3,2,2,64,256]{4,3,2,1,0:T(8,128)(2,1)} %param.5) | copy-start | bytes 1179652
  19.8 77.0 %all-to-all-start = ((bf16[2,16,64,512]{3,2,0,1:T(8,128)(2,1)}), bf16[2,16,64,512]{3,2,0,1:T(8,128)(2,1)S(1)}, u32[]{:S(2)}, u32[]{:S(2)}) async-start(bf16[2,16,64,512]{3,2,0,1:T(8,128)(2,1)} %copy.11), calls=%async_computation | async-start | bytes 4194304 | tf_op jit(solution)/shard_map/all_to_all | solution.py:48
  27.3 66.3 %all-gather.10.cloned.1.call-start = ((), (), s32[]{:S(2)}) async-start(), calls=%async_computation.3 | async-start | bytes 1179648 | tf_op jit(solution)/shard_map/all_gather | solution.py:53
  96.8 1.0 copy-start
  111.7 67.5 %all-to-all-start.1 = ((bf16[2,16,64,512]{3,2,0,1:T(8,128)(2,1)}), bf16[2,16,64,512]{3,2,0,1:T(8,128)(2,1)S(1)}, u32[]{:S(2)}, u32[]{:S(2)}) async-start(bf16[2,16,64,512]{3,2,0,1:T(8,128)(2,1)} %copy.14), calls=%async_computation.1 | async-start | bytes 4194304 | tf_op jit(solution)/shard_map/all_to_all | solution.py:48
  115.4 60.6 %all-gather.12.cloned.1.call-start = ((), (), s32[]{:S(2)}) async-start(), calls=%async_computation.4 | async-start | bytes 1179648 | tf_op jit(solution)/shard_map/all_gather | solution.py:53
  179.2 1.0 copy-start.1
  193.8 67.7 %all-to-all-start.2 = ((bf16[2,16,64,512]{3,2,0,1:T(8,128)(2,1)}), bf16[2,16,64,512]{3,2,0,1:T(8,128)(2,1)S(1)}, u32[]{:S(2)}, u32[]{:S(2)}) async-start(bf16[2,16,64,512]{3,2,0,1:T(8,128)(2,1)} %copy.17), calls=%async_computation.2 | async-start | bytes 4194304 | tf_op jit(solution)/shard_map/all_to_all | solution.py:48
  197.7 60.6 %all-gather.14.cloned.1.call-start = ((), (), s32[]{:S(2)}) async-start(), calls=%async_computation.5 | async-start | bytes 1179648 | tf_op jit(solution)/shard_map/all_gather | solution.py:53
  261.5 1.0 copy-start.2
Sparse Core Ops, SparseCore 0:
  42.7 50.9 all-gather.9
  118.4 57.5 all-gather.11
  200.7 57.5 all-gather.13
where the time goes:
time: 274 us; the launch traced here: 273 us
  waiting for transfers between devices  168 us (61%)
  local copies, waits for them, and re-layouts  40.8 us (15%)
  between operations  25 us (9%)
  starting transfers between devices  15.2 us (6%)
  other arithmetic  10.7 us (4%)
  matrix products  6.96 us (3%)
  blocking collectives  6.39 us (2%)
    all_gather x3, waiting for transfers between devices, shards(): lax.all_gather(branch_part, 'leg', axis=1, tiled=True)  168 us
    another operation x6, local copies, waits for them, and re-layouts, shards(): blocks = permuted.reshape(2, dev_count, row_count // dev_count, col_count)  16.1 us
    all_to_all x3, starting transfers between devices, shards(): lax.all_to_all(blocks, ('leg', 'sub'), split_axis=1, concat_axis=1, tiled...  15.1 us
    another operation x2, local copies, waits for them, and re-layouts, permute_legs(): split = flat.reshape(lead + (2,) * high_bits + (low_size,))  7.88 us
    dot_general x3, matrix products, fold_rows(): jnp.dot(operand, complex_matrix(shard_piece), preferred_element_type=jnp....  6.96 us
    all_gather x3, blocking collectives, shards(): branch_part = lax.all_gather(chosen, 'sub', axis=2, tiled=True)  6.39 us
    squeeze x3, local copies, waits for them, and re-layouts, complex_matrix(): imag_part = complex_block[1]  6.19 us
    transpose x2, other arithmetic, permute_legs(): return jnp.transpose(split, axes).reshape(flat.shape)  5.93 us
  transfers between devices with their start and end apart: 6, of which 3 were waited for; matrix products, arithmetic and copies ran while one was open for 4% of the time, Pallas kernels for 0%

commit v1 on v0

--- a/solution.py
+++ b/solution.py
@@ -1,9 +1,12 @@
 import jax
 import jax.numpy as jnp
 from jax import lax
+from jax.experimental import pallas as pl
+from jax.experimental.pallas import tpu as pltpu
 from jax.sharding import PartitionSpec as P
 
 STEPS = 3
+MESH = pl.DeviceIdType.MESH
 
 
 def permute_legs(flat, high_bits, low_size, rotation):
@@ -55,6 +58,240 @@
     return current
 
 
+def follow_legs(block_bits, high_bits):
+    block = ["D%d" % i for i in range(block_bits)]
+    local = ["H%d" % i for i in range(high_bits)]
+    summed = []
+    for step in range(STEPS):
+        local = [local[(b + 2 * step + 3) % high_bits] for b in range(high_bits)]
+        lead = local[high_bits - block_bits :]
+        local = local[: high_bits - block_bits] + block
+        block = lead
+        summed.append(tuple(local[:2]))
+        local[:2] = ["ABC"[step] + "0", "ABC"[step] + "1"]
+    return summed, block, local
+
+
+def stays_home(block_count, rows, cols):
+    high_bits = (rows * 4).bit_length() - 1
+    block_bits = block_count.bit_length() - 1
+    if cols != 512 or rows != 1024 or block_bits > high_bits:
+        return False
+    summed, block, local = follow_legs(block_bits, high_bits)
+    return (
+        summed == [("H3", "H4"), ("H8", "H9"), ("A0", "H11")]
+        and block == ["D%d" % i for i in range(block_bits)]
+        and local == ["C0", "C1", "H0", "H1", "H2", "B0", "B1", "H10", "A1", "H5", "H6", "H7"]
+    )
+
+
+CHUNKS = 4
+PART = 256
+
+
+def tile(values, row, col):
+    return values[col // 2][row : row + 8, (col % 2) * 128 : (col % 2 + 1) * 128]
+
+
+def gather_rows(xs, lhs, g):
+    for q in range(2):
+        for m in range(4):
+            pieces = []
+            for r in range(32):
+                h9, h8, h11, h5, h10 = [(r >> s) & 1 for s in (4, 3, 2, 1, 0)]
+                h = (h11 << 11) + (h10 << 10) + (h9 << 9) + (h8 << 8) + (g << 6) + (h5 << 5) + (m << 3)
+                pieces.append(xs[q, h : h + 8, :])
+            col = q * 4 + m
+            lhs[g, :, col * 128 : (col + 1) * 128] = jnp.concatenate(pieces, 0).astype(jnp.bfloat16)
+
+
+def next_rows_0(values, q, lhs, g):
+    for m in range(4):
+        pieces = []
+        for r in range(32):
+            h11, a0, h5, a1, h10 = [(r >> s) & 1 for s in (4, 3, 2, 1, 0)]
+            pieces.append(tile(values, m * 64 + (h11 * 4 + h5 * 2 + h10) * 8, a1 * 2 + a0))
+        col = q * 4 + m
+        lhs[g, :, col * 128 : (col + 1) * 128] = jnp.concatenate(pieces, 0).astype(jnp.bfloat16)
+
+
+def next_rows_1(values, q, lhs, g):
+    for m in range(4):
+        pieces = []
+        for r in range(32):
+            row, b = r >> 2, r & 3
+            pieces.append(tile(values, m * 64 + row * 8, b))
+        col = q * 4 + m
+        lhs[g, :, col * 128 : (col + 1) * 128] = jnp.concatenate(pieces, 0).astype(jnp.bfloat16)
+
+
+def kernel(order_in, cut_in, stem, shard_in, out, order, cut, shard, x, xs, lhs_a, lhs_b, held, neg, result, in_sem, out_sem, send, recv):
+    leg = lax.axis_index("leg")
+    sub = lax.axis_index("sub")
+    spot = leg // 2 + (leg % 2) * (7 - 2 * (leg // 2))
+
+    def leg_at(place):
+        place = lax.rem(place + 16, 8)
+        far = place // 4
+        return far * (15 - 2 * place) + (1 - far) * 2 * place
+
+    after = dict(leg=leg_at(spot + 1), sub=sub)
+    before = dict(leg=leg_at(spot - 1), sub=sub)
+    sibling = dict(leg=leg, sub=1 - sub)
+
+    barrier = pltpu.get_barrier_semaphore()
+    for peer in (after, before, sibling):
+        pl.semaphore_signal(barrier, inc=1, device_id=peer, device_id_type=MESH)
+
+    loads = [
+        pltpu.make_async_copy(source, target, in_sem.at[i])
+        for i, (source, target) in enumerate(((order_in, order), (cut_in, cut), (shard_in, shard), (stem, x)))
+    ]
+    for load in loads:
+        load.start()
+    for load in loads[:3]:
+        load.wait()
+    for step in range(STEPS):
+        chosen = shard[order[step], cut[step]]
+        held[step, sub, leg, 0] = chosen[1]
+        held[step, sub, leg, 1] = chosen[0]
+    pl.semaphore_wait(barrier, 3)
+
+    def copy(ref, step, slot, target):
+        return pltpu.make_async_remote_copy(
+            src_ref=ref,
+            dst_ref=ref,
+            send_sem=send.at[step, slot],
+            recv_sem=recv.at[step, slot],
+            device_id=target,
+            device_id_type=MESH,
+        )
+
+    def block(step, way, dist, side):
+        owner = leg_at(spot - dist if way == 0 else spot + dist)
+        if dist == 4:
+            return held.at[step, side, owner, way]
+        return held.at[step, side, owner]
+
+    def ring(step, way, dist, sending):
+        target = after if way == 0 else before
+        if sending and dist == 4:
+            owner = leg_at(spot - 3 if way == 0 else spot + 3)
+            ref = held.at[step, sub, owner, way]
+        else:
+            ref = block(step, way, dist - 1 if sending else dist, sub)
+        return copy(ref, step, way * 4 + dist - 1, target)
+
+    def share(step, way, dist, sending):
+        slot = 8 if dist == 0 else 8 + way * 4 + dist
+        return copy(block(step, way, dist, sub if sending else 1 - sub), step, slot, sibling)
+
+    def send_own(step):
+        for way in range(2):
+            ring(step, way, 1, True).start()
+        share(step, 0, 0, True).start()
+
+    def take(step, dist):
+        for way in range(2):
+            ring(step, way, dist, False).wait_recv()
+            if dist < 4:
+                ring(step, way, dist + 1, True).start()
+            share(step, way, dist, True).start()
+
+    def take_shared(step):
+        share(step, 0, 0, False).wait_recv()
+        for dist in range(1, 5):
+            for way in range(2):
+                share(step, way, dist, False).wait_recv()
+
+    def finish(step):
+        share(step, 0, 0, True).wait_send()
+        for dist in range(1, 5):
+            for way in range(2):
+                ring(step, way, dist, True).wait_send()
+                share(step, way, dist, True).wait_send()
+
+    for step in range(STEPS):
+        send_own(step)
+
+    loads[3].wait()
+    for q in range(2):
+        for j in range(4):
+            xs[q, pl.ds(j, 1024, 4), :] = x[q, :, j * 128 : (j + 1) * 128].astype(jnp.float32)
+    early = [(0, 1), (1, 1), (0, 2), (2, 1), (1, 2), (0, 3), (2, 2), (1, 3)]
+    for i, turn in enumerate(early):
+        take(*turn)
+        if i in (2, 3, 4, 5):
+            gather_rows(xs, lhs_a, i - 2)
+    between = {(0, 1): (2, 3), (0, 3): (1, 4), (1, 1): (2, 4)}
+
+    now, later = lhs_a, lhs_b
+    for step in range(STEPS):
+        if step == 0:
+            take(0, 4)
+        take_shared(step)
+        for side in range(2):
+            neg[side] = -held[step, side, :, 0]
+        for g in range(CHUNKS):
+            if (step, g) in between:
+                take(*between[step, g])
+            lhs = now[g]
+            re, im = [], []
+            for side in range(2):
+                mi = held[step, side, :, 0].reshape(512, 256)
+                mr = held[step, side, :, 1].reshape(512, 256)
+                w_re = jnp.concatenate([mr, neg[side].reshape(512, 256)], 0)
+                w_im = jnp.concatenate([mi, mr], 0)
+                re.append(jnp.dot(lhs, w_re, preferred_element_type=jnp.float32))
+                im.append(jnp.dot(lhs, w_im, preferred_element_type=jnp.float32))
+            if step < STEPS - 1:
+                arrange = next_rows_0 if step == 0 else next_rows_1
+                arrange(re, 0, later, g)
+                arrange(im, 1, later, g)
+            else:
+                rows = pl.ds(g * PART, PART)
+                for side in range(2):
+                    result[0, rows, side * 256 : (side + 1) * 256] = re[side].astype(jnp.bfloat16)
+                    result[1, rows, side * 256 : (side + 1) * 256] = im[side].astype(jnp.bfloat16)
+                pltpu.make_async_copy(result.at[:, rows], out.at[:, rows], out_sem.at[g]).start()
+        now, later = later, now
+
+    for step in range(STEPS):
+        finish(step)
+    for g in range(CHUNKS):
+        rows = pl.ds(g * PART, PART)
+        pltpu.make_async_copy(result.at[:, rows], out.at[:, rows], out_sem.at[g]).wait()
+
+
+def home(stem_tensor, branches, contraction_order, cut_values):
+    return pl.pallas_call(
+        kernel,
+        out_shape=jax.ShapeDtypeStruct(stem_tensor.shape, jnp.bfloat16),
+        in_specs=[pl.BlockSpec(memory_space=pltpu.HBM)] * 4,
+        out_specs=pl.BlockSpec(memory_space=pltpu.HBM),
+        scratch_shapes=[
+            pltpu.SMEM(contraction_order.shape, jnp.int32),
+            pltpu.SMEM(cut_values.shape, jnp.int32),
+            pltpu.VMEM(branches.shape, jnp.bfloat16),
+            pltpu.VMEM((2, 1024, 512), jnp.bfloat16),
+            pltpu.VMEM((2, 4096, 128), jnp.float32),
+            pltpu.VMEM((CHUNKS, PART, 1024), jnp.bfloat16),
+            pltpu.VMEM((CHUNKS, PART, 1024), jnp.bfloat16),
+            pltpu.VMEM((STEPS, 2, 8, 2, 64, 256), jnp.bfloat16),
+            pltpu.VMEM((2, 8, 64, 256), jnp.bfloat16),
+            pltpu.VMEM((2, 1024, 512), jnp.bfloat16),
+            pltpu.SemaphoreType.DMA((4,)),
+            pltpu.SemaphoreType.DMA((CHUNKS,)),
+            pltpu.SemaphoreType.DMA((STEPS, 8 + 9)),
+            pltpu.SemaphoreType.DMA((STEPS, 8 + 9)),
+        ],
+        compiler_params=pltpu.CompilerParams(
+            collective_id=0, has_side_effects=True, vmem_limit_bytes=62 * 1024 * 1024
+        ),
+        name="absorb",
+    )(contraction_order, cut_values, stem_tensor, branches)
+
+
 def solution(mesh):
     placed = (
         P(None, ("cuts", "leg", "sub"), None),
@@ -62,8 +299,16 @@
         P(),
         P("cuts"),
     )
+    groups = mesh.shape["leg"] * mesh.shape["sub"]
+
+    def body(stem_tensor, *rest):
+        square = mesh.shape["leg"] == 8 and mesh.shape["sub"] == 2
+        if square and stays_home(groups, stem_tensor.shape[1], stem_tensor.shape[2]):
+            return home(stem_tensor, *rest)
+        return shards(stem_tensor, *rest)
+
     return jax.shard_map(
-        shards,
+        body,
         mesh=mesh,
         in_specs=placed,
         out_specs=P(None, ("cuts", "leg", "sub"), None),

time: 274 us -> 33.1 us (0.12)
  waiting for transfers between devices: 168 us -> 0 us
  local copies, waits for them, and re-layouts: 40.8 us -> 3.05 us
  Pallas kernels: 0 us -> 29.9 us
  between operations: 25 us -> 0.01 us
  starting transfers between devices: 15.2 us -> 0 us
  other arithmetic: 10.7 us -> 0 us
  matrix products: 6.96 us -> 0 us
  blocking collectives: 6.39 us -> 0 us
    all_gather x3 -> x0, waiting for transfers between devices: 168 us -> none  [shards(): lax.all_gather(branch_part, 'leg', axis=1, tiled=True)]
    pallas_call x0 -> x1, Pallas kernels: none -> 29.9 us  [home(): pl.pallas_call(kernel, out_shape=jax.ShapeDtypeStruct(stem_tensor.shape,...]
    another operation x17 -> x0, local copies, waits for them, and re-layouts: 29.9 us -> none  [the longest x6 16.1 us: shards(): blocks = permuted.reshape(2, dev_count, row_count // dev_count, col_count)]
    all_to_all x3 -> x0, starting transfers between devices: 15.1 us -> none  [shards(): lax.all_to_all(blocks, ('leg', 'sub'), split_axis=1, concat_axis=1, tiled...]
    dot_general x3 -> x0, matrix products: 6.96 us -> none  [fold_rows(): jnp.dot(operand, complex_matrix(shard_piece), preferred_element_type=jnp....]
    all_gather x3 -> x0, blocking collectives: 6.39 us -> none  [shards(): branch_part = lax.all_gather(chosen, 'sub', axis=2, tiled=True)]
    squeeze x3 -> x0, local copies, waits for them, and re-layouts: 6.19 us -> none  [complex_matrix(): imag_part = complex_block[1]]
    transpose x2 -> x0, other arithmetic: 5.93 us -> none  [permute_legs(): return jnp.transpose(split, axes).reshape(flat.shape)]
  transfers between devices with their start and end apart: 6 -> 0, of which waited for: 3 -> 0; matrix products, arithmetic and copies ran while one was open for 4% -> 0% of each run, Pallas kernels for 0% -> 0%
where the time goes in v1:
time: 33.1 us; the launch traced here: 32.9 us
  Pallas kernels  29.9 us (90%)
  local copies, waits for them, and re-layouts  3.05 us (9%)
    pallas_call x1, Pallas kernels, home(): pl.pallas_call(kernel, out_shape=jax.ShapeDtypeStruct(stem_tensor.shape,...  29.9 us
    unnamed x1, local copies, waits for them, and re-layouts  3.05 us

profile of v1, /device:TPU:0, one launch (start us, length us, event | category | flops | bytes accessed | tf_op | source)
XLA Modules:
  0.0 32.9 jit_solution(17674177030543609458)
XLA Ops:
  0.0 29.9 %absorb.1 = bf16[2,1024,512]{2,1,0:T(8,128)(2,1)} custom-call(s32[3]{0:T(128)} %order_in.1, s32[3]{0:T(128)} %cut_in.1, bf16[2,1024,512]{2,1,0:T(8,128)(2,1)} %stem.1, bf16[3,2,2,64,256]{4,3,2,1,0:T(8,128)(2,1)} %shard_in.1), custom_call_target="tpu_custom_call" | custom-call | tf_op jit(solution)/shard_map/absorb/pallas_call | solution.py:267
  29.9 3.0 %copy.6 = bf16[2,1024,512]{2,1,0:T(8,128)(2,1)} copy(bf16[2,1024,512]{2,1,0:T(8,128)(2,1)} %absorb.1) | data formatting | bytes 4194304
